TPU v7x, 512 devices: a whole 4x8x8 slice. The times are simulated.
512 devices in a mesh: tm: 16 (over y, core), seq: 32 (over z, x).
Axes of the slice: x: 4, y: 8, z: 8, core: 2. Of those that a mesh axis runs over, the one named last changes fastest.
Arguments:
- trajectory: bfloat16 [16, 4, 1024, 3072], P('tm', None, 'seq'), may hold values from -6 to 6
- plan: int32 [16], P('tm'), may hold values from 0 to 15
- step_sizes: float32 [16], P('tm'), may hold values from 0.05 to 0.5
- modulation: bfloat16 [16, 2, 3, 3072], replicated, may hold values from -3 to 3
- q_gain: float32 [2, 3072], replicated, may hold values from -3.2 to 3.2
- k_gain: float32 [2, 3072], replicated, may hold values from -3.2 to 3.2
- tile_mask: int32 [24, 8, 8], replicated, may hold values from 0 to 1, as said below
Outputs:
- displacement: float32 [16, 4, 1024, 3072], P('tm', None, 'seq')
Inputs may be any that keep to these rules, and one draw needn't show every extreme that they name: `tile_mask`: every diagonal tile is kept.
All inputs are finite; a program needn't handle non-finite values.
Results may differ from a plain program's by a relative error of at most 0.0095.
Values may be sent and summed in bfloat16 or wider, within the bound.
A program may use at most 128 MiB of HBM per device.

v0:
```python
import jax
import jax.numpy as jnp
from jax import lax
from jax.sharding import PartitionSpec as P

TXT = 512
IMG_W = 64


def entering(value, axis, combine, identity):
    size, mine = (lax.axis_size(axis), lax.axis_index(axis))
    everything = lax.all_gather(value, axis)
    start = jnp.broadcast_to(jnp.asarray(identity, value.dtype), value.shape)

    def step(k, before):
        reached = k < mine
        new = combine(before, everything[k])
        return jnp.where(reached, new, before)

    return lax.fori_loop(0, size, step, start)


def rope_tables(positions, head):
    half = head // 2
    first = head // 16
    second = (half - first) // 2
    image = positions - TXT
    is_image = positions >= TXT
    row_pos = jnp.where(is_image, image // IMG_W, 0).astype(jnp.float32)
    col_pos = jnp.where(is_image, image % IMG_W, 0).astype(jnp.float32)
    freqs = 10000.0 ** (-(jnp.arange(second, dtype=jnp.float32) / second))
    angles = jnp.concatenate(
        [
            jnp.zeros((positions.shape[0], first), jnp.float32),
            row_pos[:, None] * freqs[None],
            col_pos[:, None] * freqs[None],
        ],
        axis=1,
    )
    return (jnp.cos(angles), jnp.sin(angles))


def rotate(values, cosine, sine):
    pairs = values.reshape(values.shape[:-1] + (values.shape[-1] // 2, 2))
    first_part = pairs[..., 0]
    second_part = pairs[..., 1]
    turned = jnp.stack(
        [first_part * cosine - second_part * sine, first_part * sine + second_part * cosine], -1
    )
    return turned.reshape(values.shape)


def head_norm(values, gain):
    return values * lax.rsqrt(jnp.mean(values * values, axis=-1, keepdims=True) + 1e-06) * gain


def select_rows(table_rows, stream, column):
    return jnp.where(stream[:, None] == 0, table_rows[0, column][None], table_rows[1, column][None])


def modulate(rows, table_rows, stream):
    values = rows.astype(jnp.float32)
    center = jnp.mean(values, axis=-1, keepdims=True)
    spread = jnp.mean((values - center) ** 2, axis=-1, keepdims=True)
    normed = (values - center) * lax.rsqrt(spread + 1e-06)
    shifted = normed * (1.0 + select_rows(table_rows, stream, 1)) + select_rows(
        table_rows, stream, 0
    )
    return (shifted.astype(jnp.bfloat16), select_rows(table_rows, stream, 2))


def attend_rows(query, keys, values, mask_rows, tile):
    scores = jnp.dot(query, keys.T, preferred_element_type=jnp.float32) * query.shape[-1] ** (-0.5)
    factor, tiles_n = mask_rows.shape
    scores = scores.reshape(factor, tile, tiles_n, tile)
    scores = jnp.where(mask_rows[:, None, :, None] > 0, scores, -1e30).reshape(
        factor * tile, tiles_n * tile
    )
    top = jnp.max(scores, axis=-1, keepdims=True)
    weights = jnp.exp(scores - top)
    weights = (weights / jnp.sum(weights, axis=-1, keepdims=True)).astype(jnp.bfloat16)
    return jnp.dot(weights, values, preferred_element_type=jnp.float32).astype(jnp.bfloat16)


def attend(query, keys, values, mask_tiles, tile):
    tiles_n = mask_tiles.shape[0]
    factor = 4
    blocks = tiles_n // factor
    block_rows = factor * tile
    query_blocks = query.reshape(blocks, block_rows, query.shape[-1])
    mask_blocks = mask_tiles.reshape(blocks, factor, tiles_n)
    result = lax.map(
        lambda pair: attend_rows(pair[0], keys, values, pair[1], tile), (query_blocks, mask_blocks)
    )
    return result.reshape(query.shape)


def add_terms(earlier, later):
    return earlier + later


def body(trajectory, plan, step_sizes, modulation, q_gain, k_gain, tile_mask):
    groups = lax.axis_size("seq")
    place = lax.axis_index("seq")
    rows = trajectory[0]
    batch, local, width = rows.shape
    heads_n = tile_mask.shape[0]
    head = width // heads_n
    total = local * groups
    per_dev = batch * heads_n // groups
    tile = total // tile_mask.shape[-1]
    local_pos = place * local + jnp.arange(local, dtype=jnp.int32)
    local_stream = (local_pos >= TXT).astype(jnp.int32)
    table_rows = modulation[plan[0]].astype(jnp.float32)
    shifted, gate = modulate(rows, table_rows, local_stream)
    item_head = (place * per_dev + jnp.arange(per_dev, dtype=jnp.int32)) % heads_n
    head_pick = (item_head[:, None] == jnp.arange(heads_n, dtype=jnp.int32)[None]).astype(
        jnp.float32
    )

    def to_items(values):
        return values.transpose(0, 2, 1, 3).reshape(groups, per_dev, local, head)

    q_tok = jnp.where(local_stream[:, None] == 0, q_gain[0][None], q_gain[1][None]).reshape(
        local, heads_n, head
    )
    k_tok = jnp.where(local_stream[:, None] == 0, k_gain[0][None], k_gain[1][None]).reshape(
        local, heads_n, head
    )
    cosine, sine = rope_tables(local_pos, head)
    heads = shifted.reshape(batch, local, heads_n, head)
    values32 = heads.astype(jnp.float32)
    query = rotate(head_norm(values32, q_tok), cosine[:, None], sine[:, None]).astype(jnp.bfloat16)
    keys = rotate(head_norm(values32, k_tok), cosine[:, None], sine[:, None]).astype(jnp.bfloat16)
    query, keys, values = (
        lax.all_to_all(to_items(query), "seq", split_axis=0, concat_axis=2, tiled=True),
        lax.all_to_all(to_items(keys), "seq", split_axis=0, concat_axis=2, tiled=True),
        lax.all_to_all(to_items(heads), "seq", split_axis=0, concat_axis=2, tiled=True),
    )
    query, keys, values = (query[0], keys[0], values[0])
    masks = jnp.einsum(
        "ih,hab->iab", head_pick, tile_mask.astype(jnp.float32), precision=lax.Precision.HIGHEST
    )
    attended = lax.map(
        lambda group: attend(group[0], group[1], group[2], group[3], tile),
        (query, keys, values, masks),
    )
    size = step_sizes[0]
    back = lax.all_to_all(attended[None], "seq", split_axis=2, concat_axis=0, tiled=True)
    merged = (
        back.reshape(batch, heads_n, local, head)
        .transpose(0, 2, 1, 3)
        .reshape(batch, local, width)
        .astype(jnp.float32)
    )
    term = size * gate * merged
    before = entering(term, "tm", add_terms, jnp.zeros_like(term))
    result = before + term
    return result[None]


def solution(mesh):
    placed = (P("tm", None, "seq", None), P("tm"), P("tm"), P(), P(), P(), P())
    return jax.shard_map(
        body, mesh=mesh, in_specs=placed, out_specs=P("tm", None, "seq", None), check_vma=False
    )
```

profile of v0, /device:TPU:1, one launch (start us, length us, event | category | flops | bytes accessed | tf_op | source)
XLA Modules:
  0.0 422.8 jit_solution(15439848367631017927)
XLA Ops:
  6.5 1.4 convert_reduce_fusion
  7.9 1.3 convert_element_type.147
  9.2 3.5 copy.44
  13.4 0.8 bitcast_convert_fusion
  15.7 1.4 multiply_reduce_fusion
  18.0 1.6 broadcast_in_dim.187
  19.6 1.7 broadcast_in_dim.189
  21.3 1.7 broadcast_in_dim.191
  23.1 1.6 broadcast_in_dim.202
  24.7 1.6 broadcast_in_dim.204
  26.4 1.7 broadcast_in_dim.207
  28.0 1.6 broadcast_in_dim.209
  29.7 17.0 %broadcast_select_fusion.1 = (f32[32,24,64,2]{0,3,2,1:T(2,128)}, f32[32,24,64,2]{0,3,2,1:T(2,128)S(1)}, f32[32,24,64,2]{0,3,2,1:T(2,128)S(1)}, f32[32,24,64,2]{0,3,2,1:T(2,128)S(1)}) fusion(pred[32]{0:T(512)(128)(4,1)S(1)} %convert_compare_fusion, f32[24,64,2]{2,1,0:T(8,128)} %broadcast_in_dim.204, f32[24,64,2]{2,1,0:T(8,128)} %broadcast_in_dim.202, ...), kind=kLoop, calls=%fused_computation.43 | loop fusion | flops 491520 | bytes 1671200 | tf_op jit(solution)/shard_map/jit(_where)/select_n | solution.py:124
  46.7 7.7 %fusion.7 = (f32[4,32,24,64,2]{1,4,3,2,0:T(2,128)}, bf16[4,32,24,64,2]{1,4,3,2,0:T(2,128)(2,1)}) fusion(f32[32,24,64,2]{0,3,2,1:T(2,128)S(1)} %get-tuple-element.261, f32[4,32,24]{1,2,0:T(8,128)S(1)} %add_rsqrt_fusion, f32[32,24,64,2]{0,3,2,1:T(2,128)S(1)} %get-tuple-element.260, f32[32,24,64,2]{0,3,2,1:T(2,128)S(1)} %get-tuple-element.262, ...), kind=kLoop, calls=%fused_computation.19 | loop fusion | flops 3145728 | bytes 5125120 | tf_op jit(solution)/shard_map/mul | solution.py:54
  54.5 9.3 %fusion.8 = f32[4,32,24,64,2]{1,4,3,2,0:T(2,128)} fusion(bf16[4,32,24,64,2]{1,4,3,2,0:T(2,128)(2,1)} %get-tuple-element.236, f32[32,24,64,2]{0,3,2,1:T(2,128)} %get-tuple-element.259, f32[4,32,24]{1,2,0:T(8,128)S(1)} %add_rsqrt_fusion), kind=kLoop, calls=%fused_computation.20 | loop fusion | flops 1179648 | bytes 2764800 | tf_op jit(solution)/shard_map/mul | solution.py:54
  64.0 19.6 %subtract_convert_fusion = (bf16[4,32,24,64,1]{1,4,3,2,0:T(2,128)(2,1)S(1)}, bf16[4,32,24,64,1]{1,4,3,2,0:T(2,128)(2,1)S(1)}, bf16[4,32,24,64,1]{1,4,3,2,0:T(2,128)(2,1)S(1)}, bf16[4,32,24,64,1]{1,4,3,2,0:T(2,128)(2,1)}) fusion(f32[4,32,24,64,2]{1,4,3,2,0:T(2,128)} %get-tuple-element.235, f32[32,64]{0,1:T(8,128)S(1)} %get-tuple-element.256, ...), kind=kLoop, calls=%fused_computation.25 | loop fusion | flops 3145728 | bytes 4734976 | tf_op jit(solution)/shard_map/convert.11
  83.6 8.3 %pad_maximum_fusion.1 = bf16[4,32,24,64,2]{1,4,3,2,0:T(2,128)(2,1)S(1)} fusion(bf16[4,32,24,64,1]{1,4,3,2,0:T(2,128)(2,1)S(1)} %get-tuple-element.244, bf16[4,32,24,64,1]{1,4,3,2,0:T(2,128)(2,1)S(1)} %get-tuple-element.243), kind=kLoop, calls=%fused_computation.23 | loop fusion | flops 1572864 | bytes 1572864 | tf_op jit(solution)/shard_map/stack | solution.py:47
  92.0 5.3 %copy.49 = bf16[4,32,24,64,2]{1,2,4,3,0:T(8,128)(2,1)} copy(bf16[4,32,24,64,2]{1,4,3,2,0:T(2,128)(2,1)S(1)} %pad_maximum_fusion.1) | data formatting | bytes 1572864 | tf_op jit(solution)/shard_map/stack | solution.py:47
  97.3 4.2 copy.50
  101.5 14.1 %all-to-all-start.1 = ((bf16[32,3,32,128]{3,2,1,0:T(8,128)(2,1)}), bf16[32,3,32,128]{3,2,1,0:T(8,128)(2,1)}, u32[]{:S(2)}, u32[]{:S(2)}) async-start(bf16[32,3,32,128]{3,2,1,0:T(8,128)(2,1)} %bitcast.154), calls=%async_computation.1 | async-start | bytes 1572864 | tf_op jit(solution)/shard_map/all_to_all | solution.py:137
  115.5 9.4 %pad_maximum_fusion = bf16[4,32,24,64,2]{1,4,3,2,0:T(2,128)(2,1)S(1)} fusion(bf16[4,32,24,64,1]{1,4,3,2,0:T(2,128)(2,1)S(1)} %get-tuple-element.253, bf16[4,32,24,64,1]{1,4,3,2,0:T(2,128)(2,1)} %get-tuple-element.254), kind=kLoop, calls=%fused_computation.22 | loop fusion | flops 1572864 | bytes 1572864 | tf_op jit(solution)/shard_map/stack | solution.py:47
  125.0 3.6 copy.46
  128.6 2.7 copy.47
  131.3 5.0 %all-to-all-done.1 = bf16[32,3,32,128]{3,2,1,0:T(8,128)(2,1)} async-done(((bf16[32,3,32,128]{3,2,1,0:T(8,128)(2,1)}), bf16[32,3,32,128]{3,2,1,0:T(8,128)(2,1)}, u32[]{:S(2)}, u32[]{:S(2)}) %all-to-all-start.1) | async-done | bytes 786464 | tf_op jit(solution)/shard_map/all_to_all | solution.py:137
  136.4 5.9 %all-to-all-start = ((bf16[32,3,32,128]{3,2,1,0:T(8,128)(2,1)}), bf16[32,3,32,128]{3,2,1,0:T(8,128)(2,1)S(1)}, u32[]{:S(2)}, u32[]{:S(2)}) async-start(bf16[32,3,32,128]{3,2,1,0:T(8,128)(2,1)} %bitcast.155), calls=%async_computation | async-start | bytes 1572864 | tf_op jit(solution)/shard_map/all_to_all | solution.py:136
  142.3 1.0 copy.52
  143.3 18.7 %all-to-all-done = bf16[32,3,32,128]{3,2,1,0:T(8,128)(2,1)S(1)} async-done(((bf16[32,3,32,128]{3,2,1,0:T(8,128)(2,1)}), bf16[32,3,32,128]{3,2,1,0:T(8,128)(2,1)S(1)}, u32[]{:S(2)}, u32[]{:S(2)}) %all-to-all-start) | async-done | bytes 786464 | tf_op jit(solution)/shard_map/all_to_all | solution.py:136
  162.0 6.6 %all-to-all-start.2 = ((bf16[32,3,32,128]{3,2,1,0:T(8,128)(2,1)}), bf16[32,3,32,128]{3,2,1,0:T(8,128)(2,1)S(1)}, u32[]{:S(2)}, u32[]{:S(2)}) async-start(bf16[32,3,32,128]{3,2,1,0:T(8,128)(2,1)} %bitcast.34), calls=%async_computation.2 | async-start | bytes 1572864 | tf_op jit(solution)/shard_map/all_to_all | solution.py:138
  169.0 1.2 copy.51
  170.3 18.0 %all-to-all-done.2 = bf16[32,3,32,128]{3,2,1,0:T(8,128)(2,1)S(1)} async-done(((bf16[32,3,32,128]{3,2,1,0:T(8,128)(2,1)}), bf16[32,3,32,128]{3,2,1,0:T(8,128)(2,1)S(1)}, u32[]{:S(2)}, u32[]{:S(2)}) %all-to-all-start.2) | async-done | bytes 786464 | tf_op jit(solution)/shard_map/all_to_all | solution.py:138
  188.4 0.9 copy-done.1
  189.2 1.2 copy.53
  190.4 14.8 %while.35 = (s32[]{:T(128)}, bf16[3,1024,128]{2,1,0:T(8,128)(2,1)}, bf16[3,1024,128]{2,1,0:T(8,128)(2,1)S(1)}, f32[3,8,8]{2,0,1:T(4,128)S(1)}, bf16[3,1024,128]{...) while((s32[]{:T(128)}, bf16[3,1024,128]{2,1,0:T(8,128)(2,1)}, ...), condition=%wide.region_8.9_spmd, body=%wide.region_3.8_spmd.sunk | while | flops 272694304 | bytes 10235330 | solution.py:144
  190.6 4.1 while.37
  194.6 0.7 bitcast_dynamic-update-slice_fusion.2
  195.5 4.1 while.37
  199.5 0.7 bitcast_dynamic-update-slice_fusion.2
  200.4 4.1 while.37
  204.5 0.7 bitcast_dynamic-update-slice_fusion.2
  205.2 2.8 copy.67
  208.0 6.6 %all-to-all-start.3 = ((bf16[1,3,1024,128]{3,1,0,2:T(4,128)(2,1)}), bf16[1,3,1024,128]{3,1,0,2:T(4,128)(2,1)S(1)}, u32[]{:S(2)}, u32[]{:S(2)}) async-start(bf16[1,3,1024,128]{3,1,0,2:T(4,128)(2,1)} %bitcast.108), calls=%async_computation.3 | async-start | bytes 2097152 | tf_op jit(solution)/shard_map/all_to_all | solution.py:149
  215.4 24.0 %all-to-all-done.3 = bf16[1,3,1024,128]{3,1,0,2:T(4,128)(2,1)S(1)} async-done(((bf16[1,3,1024,128]{3,1,0,2:T(4,128)(2,1)}), bf16[1,3,1024,128]{3,1,0,2:T(4,128)(2,1)S(1)}, u32[]{:S(2)}, u32[]{:S(2)}) %all-to-all-start.3) | async-done | bytes 786464 | tf_op jit(solution)/shard_map/all_to_all | solution.py:149
  239.8 2.1 copy.58
  241.9 1.5 reshape.480
  243.4 1.3 broadcast_multiply_fusion
  244.7 138.4 %all-gather.2.cloned.1.call-done = f32[16,4,32,3072]{3,2,1,0:T(8,128)} async-done(((f32[1,4,32,3072]{3,2,1,0:T(8,128)}), f32[16,4,32,3072]{3,2,1,0:T(8,128)}) %all-gather.2.cloned.1.call-update) | async-done | bytes 25165840 | tf_op jit(solution)/shard_map/all_gather | solution.py:12
  383.1 31.6 %while.36 = (s32[]{:T(128)}, f32[4,32,3072]{2,1,0:T(8,128)S(1)}, s32[]{:T(128)}, f32[16,4,32,3072]{3,2,1,0:T(8,128)}, s32[]{:T(128)}, /*index=5*/s32[]{:T(128)}) while((s32[]{:T(128)}, f32[4,32,3072]{2,1,0:T(8,128)S(1)}, s32[]{:T(128)}, f32[16,4,32,3072]{3,2,1,0:T(8,128)}, s32[]{:T(128)}, /*index=5*/s32[]{:T(128)}) %tuple.104), condition=%wide.region_10.11_spmd.clone, body=%wide.region_9.10_spmd.clone.sunk | while | flops 1179652 | bytes 4718685 | solution.py:20
  383.1 1.9 add_select_fusion.2
  385.1 1.9 add_select_fusion.2
  387.0 1.9 add_select_fusion.2
  389.0 1.9 add_select_fusion.2
  391.0 1.9 add_select_fusion.2
  393.0 1.9 add_select_fusion.2
  394.9 1.9 add_select_fusion.2
  396.9 1.9 add_select_fusion.2
  398.9 1.9 add_select_fusion.2
  400.9 1.9 add_select_fusion.2
  402.8 1.9 add_select_fusion.2
  404.8 1.9 add_select_fusion.2
  406.8 1.9 add_select_fusion.2
  408.8 1.9 add_select_fusion.2
  410.7 1.9 add_select_fusion.2
  412.7 1.9 add_select_fusion.2
  414.7 1.3 fusion.14
  (88 shorter events, 16.0 us)
Async XLA Ops:
  6.5 2.7 copy-start
  17.1 5.9 %copy-start.4 = (f32[2,3072]{1,0:T(2,128)S(1)}, f32[2,3072]{1,0:T(2,128)}, u32[]{:S(2)}) copy-start(f32[2,3072]{1,0:T(2,128)} %param.18) | copy-start | bytes 73732
  17.1 5.9 %copy-start.5 = (f32[2,3072]{1,0:T(2,128)S(1)}, f32[2,3072]{1,0:T(2,128)}, u32[]{:S(2)}) copy-start(f32[2,3072]{1,0:T(2,128)} %param.17) | copy-start | bytes 73732
  28.0 18.6 %slice-start = ((s8[6291456]{0:T(1024)(128)(4,1)}), s8[2097152]{0:T(1024)(128)(4,1)S(1)}, s32[]{:S(2)}) async-start(s8[6291456]{0:T(1024)(128)(4,1)} %bitcast.136), calls=%async_computation.5 | async-start | bytes 4194304
  29.7 17.0 %slice-start.1 = ((s8[6291456]{0:T(1024)(128)(4,1)}), s8[4194304]{0:T(1024)(128)(4,1)S(1)}, s32[]{:S(2)}) async-start(s8[6291456]{0:T(1024)(128)(4,1)} %bitcast.136), calls=%async_computation.6 | async-start | bytes 8388608
  101.5 34.9 %all-to-all-start.1 = ((bf16[32,3,32,128]{3,2,1,0:T(8,128)(2,1)}), bf16[32,3,32,128]{3,2,1,0:T(8,128)(2,1)}, u32[]{:S(2)}, u32[]{:S(2)}) async-start(bf16[32,3,32,128]{3,2,1,0:T(8,128)(2,1)} %bitcast.154), calls=%async_computation.1 | async-start | bytes 1572864 | tf_op jit(solution)/shard_map/all_to_all | solution.py:137
  131.3 10.9 %copy-start.2 = (bf16[4,32,24,128]{3,2,1,0:T(8,128)(2,1)S(1)}, bf16[4,32,24,128]{3,2,1,0:T(8,128)(2,1)}, u32[]{:S(2)}) copy-start(bf16[4,32,24,128]{3,2,1,0:T(8,128)(2,1)} %get-tuple-element.238) | copy-start | bytes 2359300
  136.3 32.3 %copy-start.6 = (s32[24,8,8]{0,2,1:T(8,128)S(1)}, s32[24,8,8]{0,2,1:T(8,128)}, u32[]{:S(2)}) copy-start(s32[24,8,8]{0,2,1:T(8,128)} %param.19) | copy-start | bytes 18436
  136.4 25.7 %all-to-all-start = ((bf16[32,3,32,128]{3,2,1,0:T(8,128)(2,1)}), bf16[32,3,32,128]{3,2,1,0:T(8,128)(2,1)S(1)}, u32[]{:S(2)}, u32[]{:S(2)}) async-start(bf16[32,3,32,128]{3,2,1,0:T(8,128)(2,1)} %bitcast.155), calls=%async_computation | async-start | bytes 1572864 | tf_op jit(solution)/shard_map/all_to_all | solution.py:136
  162.0 26.3 %all-to-all-start.2 = ((bf16[32,3,32,128]{3,2,1,0:T(8,128)(2,1)}), bf16[32,3,32,128]{3,2,1,0:T(8,128)(2,1)S(1)}, u32[]{:S(2)}, u32[]{:S(2)}) async-start(bf16[32,3,32,128]{3,2,1,0:T(8,128)(2,1)} %bitcast.34), calls=%async_computation.2 | async-start | bytes 1572864 | tf_op jit(solution)/shard_map/all_to_all | solution.py:138
  188.3 0.9 copy-start.1
  205.2 10.1 %copy-start.3 = (f32[1,1,3072]{2,0,1:T(1,128)S(1)}, f32[1,1,3072]{2,0,1:T(1,128)}, u32[]{:S(2)}) copy-start(f32[1,1,3072]{2,0,1:T(1,128)} %get-tuple-element.248) | copy-start | bytes 36868
  208.0 31.4 %all-to-all-start.3 = ((bf16[1,3,1024,128]{3,1,0,2:T(4,128)(2,1)}), bf16[1,3,1024,128]{3,1,0,2:T(4,128)(2,1)S(1)}, u32[]{:S(2)}, u32[]{:S(2)}) async-start(bf16[1,3,1024,128]{3,1,0,2:T(4,128)(2,1)} %bitcast.108), calls=%async_computation.3 | async-start | bytes 2097152 | tf_op jit(solution)/shard_map/all_to_all | solution.py:149
  214.6 168.6 %all-gather.2.cloned.1.call-start = ((), (), s32[]{:S(2)}) async-start(), calls=%async_computation.4 | async-start | bytes 26738688 | tf_op jit(solution)/shard_map/all_gather | solution.py:12
Sparse Core Ops, SparseCore 0:
  244.8 138.2 all-gather.1
where the time goes:
time: 424 us; the launch traced here: 423 us
  waiting for transfers between devices  204 us (48%)
  other arithmetic  114 us (27%)
  local copies, waits for them, and re-layouts  47.5 us (11%)
  starting transfers between devices  33.2 us (8%)
  between operations  15 us (4%)
  matrix products  7.96 us (2%)
    all_gather x1, waiting for transfers between devices, entering(): everything = lax.all_gather(value, axis)  138 us
    select_n x16, other arithmetic, step(): return jnp.where(reached, new, before)  31.2 us
    all_to_all x1, waiting for transfers between devices, body(): lax.all_to_all(attended[None], 'seq', split_axis=2, concat_axis=0, tiled=...  24 us
    another operation x4, other arithmetic  19.6 us
    all_to_all x1, waiting for transfers between devices, body(): lax.all_to_all(to_items(query), 'seq', split_axis=0, concat_axis=2, tiled...  18.7 us
    all_to_all x1, waiting for transfers between devices, body(): lax.all_to_all(to_items(heads), 'seq', split_axis=0, concat_axis=2, tiled...  18 us
    another operation x2, other arithmetic, rotate(): jnp.stack([first_part * cosine - second_part * sine, first_part * sine +...  17.8 us
    select_n x1, other arithmetic, body(): jnp.where(local_stream[:, None] == 0, q_gain[0][None], q_gain[1][None])  17 us
  transfers between devices with their start and end apart: 5, of which 5 were waited for; matrix products, arithmetic and copies ran while one was open for 4% of the time, Pallas kernels for 0%

commit v1 on v0

v1 whole, which is shorter than its diff:
```python
import functools

import jax
import jax.numpy as jnp
import numpy as np
from jax import lax
from jax.experimental import pallas as pl
from jax.experimental.pallas import tpu as pltpu
from jax.sharding import PartitionSpec as P

TXT = 512
IMG_W = 64
MESH = pl.DeviceIdType.MESH
F32 = jnp.float32
BF16 = jnp.bfloat16

B, H, HD, D = 4, 24, 128, 3072
L = 1024
S = 32
LOC = L // S
PER = B * H // S
HG = H // PER
HALF = L // 2
CH = 128
NCH = HALF // CH
QB = 256
NEG = -1e30


def rope_tables():
    half = HD // 2
    first = HD // 16
    second = (half - first) // 2
    image = np.arange(L - TXT)
    freqs = (np.float32(10000.0) ** (-(np.arange(second, dtype=np.float32) / np.float32(second)))).astype(np.float32)
    row = (image // IMG_W).astype(np.float32)
    col = (image % IMG_W).astype(np.float32)
    angles = np.concatenate(
        [np.zeros((L - TXT, first), np.float32), row[:, None] * freqs[None], col[:, None] * freqs[None]], axis=1
    ).astype(np.float32)
    cosine = np.repeat(np.cos(angles), 2, axis=1)
    sine = np.repeat(np.sin(angles), 2, axis=1)
    sine[:, 0::2] *= -1.0
    return cosine.astype(np.float32), sine.astype(np.float32)


def kernel(
    plan_ref,
    step_ref,
    x_ref,
    mod_ref,
    qg_ref,
    kg_ref,
    mask_ref,
    cos_ref,
    sin_ref,
    out_ref,
    send_u,
    recv_u,
    q_aug,
    k_aug,
    v_aug,
    bias,
    own,
    ex_out,
    ex_in,
    e_in,
    r_in,
    t_in,
    p_out,
    s_out,
    d_out,
    in_send,
    in_recv,
    ex_send,
    ex_recv,
    f_send,
    f_recv,
    r_send,
    r_recv,
    t_send,
    t_recv,
    o_send,
    o_recv,
):
    tm = lax.axis_index("tm")
    s = lax.axis_index("seq")
    y = tm // 2
    c = tm % 2
    x = s % 4
    image = s // HG
    head0 = (s % HG) * PER
    ypos = y % 4

    bar = pltpu.get_barrier_semaphore()

    def greet(i, carry):
        pl.semaphore_signal(bar, inc=1, device_id=(tm, lax.rem(s + i, S)), device_id_type=MESH)
        return carry

    lax.fori_loop(1, S, greet, 0)

    def greet_tm(other):
        pl.semaphore_signal(bar, inc=1, device_id=(other, s), device_id_type=MESH)

    greet_tm(y * 2 + 1 - c)
    one = jnp.int32(1)
    zero = jnp.int32(0)

    @pl.when(ypos > 0)
    def _():
        greet_tm(tm - 2)

    @pl.when(y < 3)
    def _():
        greet_tm(tm + 2)

    @pl.when((y == 4) | (y == 5))
    def _():
        greet_tm(6 + c)

    @pl.when(y >= 6)
    def _():
        greet_tm(c)

    plan = plan_ref[0]
    stream = jnp.where(s >= TXT // LOC, one, zero)
    table = mod_ref[plan, stream].astype(F32)
    shift = table[0:1]
    scale = 1.0 + table[1:2]

    def modulate(b, carry):
        rows = x_ref[b].astype(F32)
        center = jnp.mean(rows, axis=-1, keepdims=True)
        rows = rows - center
        spread = jnp.mean(rows * rows, axis=-1, keepdims=True)
        u = (rows * lax.rsqrt(spread + 1e-06) * scale + shift).astype(BF16)
        for h in range(H):
            send_u[b * HG + h // PER, h % PER] = u[:, h * HD : (h + 1) * HD]
        return carry

    lax.fori_loop(0, B, modulate, 0)

    receivers = 31 + 1 + jnp.where(ypos != 3, one, zero) + jnp.where((y >= 1) & (y <= 3), one, zero)
    receivers = receivers + jnp.where((y == 0) | (y == 3), one + one, zero)
    pl.semaphore_wait(bar, receivers)

    for j in range(PER):
        pltpu.make_async_copy(send_u.at[s, j], recv_u.at[j, s], in_recv.at[j]).start()

        def spread_u(i, carry, j=j):
            p = lax.rem(s + i, S)
            pltpu.make_async_remote_copy(
                send_u.at[p, j],
                recv_u.at[j, s],
                in_send,
                in_recv.at[j],
                device_id=(tm, p),
                device_id_type=MESH,
            ).start()
            return carry

        lax.fori_loop(1, S, spread_u, 0)

    lane = lax.broadcasted_iota(jnp.int32, (L, HD), 1)
    tile = lax.broadcasted_iota(jnp.int32, (L, HD), 0) // 128
    k_aug[:, HD:] = jnp.where(lane == tile, 1.0, 0.0).astype(BF16)
    v_aug[:, HD:] = jnp.ones((L, HD), BF16)
    bias[...] = jnp.zeros((8, HD), F32)
    lane_row = lax.broadcasted_iota(jnp.int32, (HD, HD), 0)
    lane_col = lax.broadcasted_iota(jnp.int32, (HD, HD), 1)
    partner = jnp.where(lane_col % 2 == 0, lane_col + 1, lane_col - 1)
    swap = jnp.where(lane_row == partner, 1.0, 0.0).astype(BF16)
    even = lax.broadcasted_iota(jnp.int32, (8, HD), 1) % 2 == 0
    factor = HD ** (-0.5) * 1.4426950408889634
    step = step_ref[0]

    def swapped(row):
        row = jnp.broadcast_to(row, (8, HD))
        return jnp.where(even, pltpu.roll(row, HD - 1, 1), pltpu.roll(row, 1, 1))[0:1]

    def attention(j):
        head = head0 + j
        cols = pl.ds(pl.multiple_of(head * HD, HD), HD)
        pltpu.make_async_copy(recv_u.at[j], recv_u.at[j], in_recv.at[j]).wait()
        u = recv_u[j].reshape(L, HD)
        v_aug[:, :HD] = u
        u32 = u.astype(F32)
        inv = lax.rsqrt(jnp.mean(u32 * u32, axis=-1, keepdims=True) + 1e-06)
        n32 = u32 * inv
        turned = jnp.dot(u[TXT:], swap, preferred_element_type=F32) * inv[TXT:]
        cosine = cos_ref[...]
        sine = sin_ref[...]

        def fill(target, gain_ref, extra):
            gain = gain_ref[:, cols] * extra
            target[:TXT, :HD] = (n32[:TXT] * gain[0:1]).astype(BF16)
            target[TXT:, :HD] = (
                n32[TXT:] * (cosine * gain[1:2]) + turned * (sine * swapped(gain[1:2]))
            ).astype(BF16)

        fill(q_aug, qg_ref, factor)
        fill(k_aug, kg_ref, 1.0)
        kept = mask_ref[head].astype(F32)
        bias[:, 0:8] = (1.0 - kept) * NEG
        for a in range(8):
            q_aug[a * 128 : (a + 1) * 128, HD:] = jnp.broadcast_to(bias[a : a + 1, :], (128, HD)).astype(BF16)

        gate_text = mod_ref[plan, 0, :, cols].astype(F32)[2:3] * step
        gate_image = mod_ref[plan, 1, :, cols].astype(F32)[2:3] * step

        def rows_of(start, is_image):
            query = q_aug[pl.ds(start, QB), :]
            scores = lax.dot_general(query, k_aug[...], (((1,), (1,)), ((), ())), preferred_element_type=F32)
            top = jnp.max(scores, axis=-1, keepdims=True)
            weights = jnp.exp2(scores - top).astype(BF16)
            summed = jnp.dot(weights, v_aug[...], preferred_element_type=F32)
            gate = jnp.where(is_image, gate_image, gate_text)
            return (summed[:, :HD] / summed[:, HD:]) * gate

        for n in range(HALF // QB):
            theirs = pl.multiple_of((1 - c) * HALF + n * QB, QB)
            ex_out[j, n] = rows_of(theirs, c == 0).astype(BF16)
            pltpu.make_async_remote_copy(
                ex_out.at[j, n],
                ex_in.at[j, n],
                ex_send.at[j, n],
                ex_recv.at[j, n],
                device_id=(y * 2 + 1 - c, s),
                device_id_type=MESH,
            ).start()
        for n in range(HALF // QB):
            mine = pl.multiple_of(c * HALF + n * QB, QB)
            own[j, n * QB : (n + 1) * QB] = rows_of(mine, c == 1)
        for n in range(HALF // QB):
            pltpu.make_async_remote_copy(
                ex_out.at[j, n],
                ex_in.at[j, n],
                ex_send.at[j, n],
                ex_recv.at[j, n],
                device_id=(y * 2 + 1 - c, s),
                device_id_type=MESH,
            ).wait()

    def chunk_of(i):
        return lax.rem(i + x, NCH)

    def both(j, r):
        mine = own[j, pl.ds(pl.multiple_of(r * CH, CH), CH), :]
        other = ex_in[j, r // 2, pl.ds(pl.multiple_of((r % 2) * CH, CH), CH), :].astype(F32)
        return mine, other

    def hop(src, dst, send_sem, recv_sem, to):
        return pltpu.make_async_remote_copy(src, dst, send_sem, recv_sem, device_id=(to, s), device_id_type=MESH)

    def forward_copy(g):
        return hop(p_out.at[g], e_in.at[g], f_send.at[g], f_recv.at[g], tm + 2)

    def reverse_copy(g):
        return hop(s_out.at[g], r_in.at[g], r_send.at[g], r_recv.at[g], tm - 2)

    def total_copy(src, g, n):
        to = jnp.where(y == 3, 8 + 2 * n, 14 - 2 * n) + c
        return hop(src.at[g], t_in.at[g], t_send.at[n, g], t_recv.at[g], to)

    def forward(j):
        def one_chunk(i, carry):
            r = chunk_of(i)
            g = j * NCH + r
            mine, other = both(j, r)
            total = mine + other

            @pl.when(ypos == 0)
            def _():
                p_out[g] = total.astype(BF16)

            @pl.when(ypos > 0)
            def _():
                forward_copy(g).wait_recv()
                p_out[g] = (total + e_in[g].astype(F32)).astype(BF16)

            @pl.when(ypos < 3)
            def _():
                forward_copy(g).start()

            @pl.when(y == 3)
            def _():
                total_copy(p_out, g, 0).start()
                total_copy(p_out, g, 1).start()
                s_out[g] = total.astype(BF16)
                reverse_copy(g).start()

            return carry

        lax.fori_loop(0, NCH, one_chunk, 0)

    def reverse(j):
        @pl.when(y < 3)
        def _():
            def one_chunk(i, carry):
                r = chunk_of(i)
                g = j * NCH + r
                mine, other = both(j, r)
                reverse_copy(g).wait_recv()
                s_out[g] = (mine + other + r_in[g].astype(F32)).astype(BF16)

                @pl.when(y > 0)
                def _():
                    reverse_copy(g).start()

                @pl.when(y == 0)
                def _():
                    total_copy(s_out, g, 0).start()
                    total_copy(s_out, g, 1).start()

                return carry

            lax.fori_loop(0, NCH, one_chunk, 0)

    def deliver(j):
        cols = pl.ds(pl.multiple_of((head0 + j) * HD, HD), HD)

        def one_chunk(i, carry):
            r = chunk_of(i)
            g = j * NCH + r
            mine, other = both(j, r)

            def put(before):
                after = before + mine + other
                first = before + jnp.where(c == 0, mine, other)
                d_out[0, g] = first.astype(BF16)
                d_out[1, g] = after.astype(BF16)

            @pl.when(y == 0)
            def _():
                put(jnp.zeros((CH, HD), F32))

            @pl.when((y > 0) & (y < 4))
            def _():
                put(e_in[g].astype(F32))

            @pl.when(y >= 4)
            def _():
                total_copy(p_out, g, 0).wait_recv()

            @pl.when(y == 4)
            def _():
                put(t_in[g].astype(F32))

            @pl.when(y > 4)
            def _():
                put(t_in[g].astype(F32) + e_in[g].astype(F32))

            def piece(i, carry):
                step_to = y * 2 + i // 4
                shard = c * (S // 2) + r * 4 + lax.rem(i + s // 4, 4)
                src = d_out.at[i // 4, g, pl.ds(pl.multiple_of(lax.rem(i + s // 4, 4) * LOC, LOC), LOC)]
                dst = out_ref.at[image, :, cols]
                here = (shard == s) & (step_to == tm)

                @pl.when(here)
                def _():
                    pltpu.make_async_copy(src, dst, o_recv).start()

                @pl.when(jnp.logical_not(here))
                def _():
                    pltpu.make_async_remote_copy(
                        src, dst, o_send, o_recv, device_id=(step_to, shard), device_id_type=MESH
                    ).start()

                return carry

            lax.fori_loop(0, 8, piece, 0)
            return carry

        lax.fori_loop(0, NCH, one_chunk, 0)

    attention(0)
    forward(0)
    attention(1)
    forward(1)
    reverse(0)

    @pl.when(y < 4)
    def _():
        deliver(0)

    attention(2)
    forward(2)

    @pl.when(y >= 4)
    def _():
        deliver(0)

    reverse(1)
    deliver(1)
    reverse(2)
    deliver(2)

    sent = send_u.at[pl.ds(0, S - 1)]
    pltpu.make_async_copy(sent, sent, in_send).wait()

    def drain(g, carry):
        @pl.when(ypos < 3)
        def _():
            forward_copy(g).wait_send()

        @pl.when((y >= 1) & (y <= 3))
        def _():
            reverse_copy(g).wait_send()

        @pl.when((y == 0) | (y == 3))
        def _():
            total_copy(p_out, g, 0).wait_send()
            total_copy(p_out, g, 1).wait_send()

        return carry

    lax.fori_loop(0, PER * NCH, drain, 0)
    most = d_out.at[0, :, pl.ds(0, CH - LOC)]
    pltpu.make_async_copy(d_out.at[1], d_out.at[1], o_send).wait()
    pltpu.make_async_copy(most, most, o_send).wait()
    rest = d_out.at[0, :, pl.ds(0, LOC)]
    last = d_out.at[0, pl.ds(0, 9), pl.ds(0, LOC)]
    holds_own = c == s // (S // 2)

    @pl.when(holds_own)
    def _():
        pltpu.make_async_copy(last, last, o_send).wait()

    @pl.when(jnp.logical_not(holds_own))
    def _():
        pltpu.make_async_copy(rest, rest, o_send).wait()

    pltpu.make_async_copy(out_ref, out_ref, o_recv).wait()


def body(trajectory, plan, step_sizes, modulation, q_gain, k_gain, tile_mask):
    cosine, sine = rope_tables()
    n = PER * NCH
    vmem = pl.BlockSpec(memory_space=pltpu.VMEM)
    smem = pl.BlockSpec(memory_space=pltpu.SMEM)
    dma = pltpu.SemaphoreType.DMA
    blocks = pl.pallas_call(
        kernel,
        out_shape=jax.ShapeDtypeStruct((B, LOC, D), BF16),
        in_specs=[smem, smem] + [vmem] * 7,
        out_specs=pl.BlockSpec(memory_space=pl.ANY),
        scratch_shapes=[
            pltpu.VMEM((S, PER, LOC, HD), BF16),
            pltpu.VMEM((PER, S, LOC, HD), BF16),
            pltpu.VMEM((L, 2 * HD), BF16),
            pltpu.VMEM((L, 2 * HD), BF16),
            pltpu.VMEM((L, 2 * HD), BF16),
            pltpu.VMEM((8, HD), F32),
            pltpu.VMEM((PER, HALF, HD), F32),
            pltpu.VMEM((PER, HALF // QB, QB, HD), BF16),
            pltpu.VMEM((PER, HALF // QB, QB, HD), BF16),
            pltpu.VMEM((n, CH, HD), BF16),
            pltpu.VMEM((n, CH, HD), BF16),
            pltpu.VMEM((n, CH, HD), BF16),
            pltpu.VMEM((n, CH, HD), BF16),
            pltpu.VMEM((n, CH, HD), BF16),
            pltpu.VMEM((2, n, CH, HD), BF16),
            dma,
            dma((PER,)),
            dma((PER, HALF // QB)),
            dma((PER, HALF // QB)),
            dma((n,)),
            dma((n,)),
            dma((n,)),
            dma((n,)),
            dma((2, n)),
            dma((n,)),
            dma,
            dma,
        ],
        compiler_params=pltpu.CompilerParams(
            collective_id=0, has_side_effects=True, vmem_limit_bytes=56 * 1024 * 1024
        ),
    )(plan, step_sizes, trajectory[0], modulation, q_gain, k_gain, tile_mask, jnp.asarray(cosine), jnp.asarray(sine))
    return blocks.astype(F32)[None]


def solution(mesh):
    placed = (P("tm", None, "seq", None), P("tm"), P("tm"), P(), P(), P(), P())
    return jax.shard_map(
        body, mesh=mesh, in_specs=placed, out_specs=P("tm", None, "seq", None), check_vma=False
    )
```

time: 424 us -> 94.2 us (0.22)
  the two profiles are of different devices: /device:TPU:1 before, /device:TPU:49 now
where the time goes in v1:
time: 94.2 us; the launch traced here: 93.8 us
  Pallas kernels  86.3 us (92%)
  local copies, waits for them, and re-layouts  3.81 us (4%)
  other arithmetic  2.43 us (3%)
  between operations  1.31 us (1%)
    pallas_call x1, Pallas kernels, body(): pl.pallas_call(kernel, out_shape=jax.ShapeDtypeStruct((B, LOC, D), BF16),...  86.3 us
    unnamed x2, local copies, waits for them, and re-layouts  3.81 us
    broadcast_in_dim x1, other arithmetic, body(): return blocks.astype(F32)[None]  2.43 us

profile of v1, /device:TPU:49, one launch (start us, length us, event | category | flops | bytes accessed | tf_op | source)
XLA Modules:
  0.0 93.8 jit_solution(564820027143580830)
XLA Ops:
  1.3 1.5 %copy.11.mask_ref = s32[24,8,8]{2,1,0:T(8,128)} copy(s32[24,8,8]{0,2,1:T(8,128)} %param.15) | data formatting | bytes 12288 | tf_op args[6]
  2.8 2.3 %copy.10.mod_ref = bf16[16,2,3,3072]{3,2,1,0:T(4,128)(2,1)} copy(bf16[16,2,3,3072]{3,1,2,0:T(2,128)(2,1)} %param.12) | data formatting | bytes 1179648 | tf_op args[3]
  5.1 86.3 %shard_map.91 = bf16[4,32,3072]{2,1,0:T(8,128)(2,1)} custom-call(s32[1]{0:T(128)S(6)} %copy.12.plan_ref, f32[1]{0:T(128)S(6)} %copy.13.step_ref, bf16[4,32,3072]{2,1,0:T(8,128)(2,1)} %bitcast.4, bf16[16,2,3,3072]{3,2,1,0:T(4,128)(2,1)} %copy.10.mod_ref, f32[2,3072]{1,0:T(2,128)} %qg_ref.1, f32[2,3072]{1,0:T(2,128)} %kg_ref.1, s32[24,8,8]{2,1,0:T(8,128)} %copy.11.mask_ref, ...), custom_call_target="tpu_custom_call" | custom-call | tf_op jit(solution)/shard_map/pallas_call | solution.py:444
  91.4 2.4 %bitcast_convert_fusion = f32[1,4,32,3072]{3,2,1,0:T(8,128)} fusion(bf16[4,32,3072]{2,1,0:T(8,128)(2,1)} %shard_map.91), kind=kLoop, calls=%fused_computation | loop fusion | flops 393216 | bytes 2359296 | tf_op jit(solution)/shard_map/broadcast_in_dim | solution.py:482

commit v2 on v1

--- a/solution.py
+++ b/solution.py
@@ -25,6 +25,8 @@
 NCH = HALF // CH
 QB = 256
 NEG = -1e30
+
+TO = {0: (1, 6, 7), 1: (0, 2, 3), 2: (0, 3), 3: (2, 4, 5), 4: (5,), 5: (6, 7), 6: (7,)}
 
 
 def rope_tables():
@@ -47,6 +49,14 @@
 def kernel(
     plan_ref,
     step_ref,
+    x_hbm,
+    mod_hbm,
+    qg_hbm,
+    kg_hbm,
+    mask_hbm,
+    cos_hbm,
+    sin_hbm,
+    out_ref,
     x_ref,
     mod_ref,
     qg_ref,
@@ -54,34 +64,36 @@
     mask_ref,
     cos_ref,
     sin_ref,
-    out_ref,
     send_u,
     recv_u,
     q_aug,
     k_aug,
     v_aug,
-    bias,
     own,
     ex_out,
     ex_in,
-    e_in,
+    a_in,
+    b_in,
     r_in,
     t_in,
+    c_out,
     p_out,
-    s_out,
+    t_out,
     d_out,
     in_send,
     in_recv,
     ex_send,
     ex_recv,
-    f_send,
-    f_recv,
-    r_send,
+    a_recv,
+    b_recv,
     r_recv,
+    t_recv,
+    c_send,
+    p_send,
     t_send,
-    t_recv,
     o_send,
     o_recv,
+    load,
 ):
     tm = lax.axis_index("tm")
     s = lax.axis_index("seq")
@@ -92,6 +104,23 @@
     head0 = (s % HG) * PER
     ypos = y % 4
 
+    loads = [
+        pltpu.make_async_copy(src, dst, load.at[n])
+        for n, (src, dst) in enumerate(
+            [
+                (x_hbm, x_ref),
+                (mod_hbm, mod_ref),
+                (qg_hbm, qg_ref),
+                (kg_hbm, kg_ref),
+                (mask_hbm, mask_ref),
+                (cos_hbm, cos_ref),
+                (sin_hbm, sin_ref),
+            ]
+        )
+    ]
+    for copy in loads:
+        copy.start()
+
     bar = pltpu.get_barrier_semaphore()
 
     def greet(i, carry):
@@ -104,30 +133,23 @@
         pl.semaphore_signal(bar, inc=1, device_id=(other, s), device_id_type=MESH)
 
     greet_tm(y * 2 + 1 - c)
-    one = jnp.int32(1)
     zero = jnp.int32(0)
 
-    @pl.when(ypos > 0)
-    def _():
-        greet_tm(tm - 2)
-
-    @pl.when(y < 3)
-    def _():
-        greet_tm(tm + 2)
-
-    @pl.when((y == 4) | (y == 5))
-    def _():
-        greet_tm(6 + c)
-
-    @pl.when(y >= 6)
-    def _():
-        greet_tm(c)
-
+    for sender, receivers in TO.items():
+        for receiver in receivers:
+
+            @pl.when(y == receiver)
+            def _(sender=sender):
+                greet_tm(2 * sender + c)
+
+    loads[0].wait()
+    loads[1].wait()
     plan = plan_ref[0]
-    stream = jnp.where(s >= TXT // LOC, one, zero)
-    table = mod_ref[plan, stream].astype(F32)
-    shift = table[0:1]
-    scale = 1.0 + table[1:2]
+    stream = jnp.where(s >= TXT // LOC, jnp.int32(1), zero)
+    table = mod_ref[plan].astype(F32)
+    text = stream == 0
+    shift = jnp.where(text, table[0, 0:1], table[0, 1:2])
+    scale = 1.0 + jnp.where(text, table[1, 0:1], table[1, 1:2])
 
     def modulate(b, carry):
         rows = x_ref[b].astype(F32)
@@ -141,9 +163,10 @@
 
     lax.fori_loop(0, B, modulate, 0)
 
-    receivers = 31 + 1 + jnp.where(ypos != 3, one, zero) + jnp.where((y >= 1) & (y <= 3), one, zero)
-    receivers = receivers + jnp.where((y == 0) | (y == 3), one + one, zero)
-    pl.semaphore_wait(bar, receivers)
+    expected = S - 1 + 1
+    for sender, receivers in TO.items():
+        expected = expected + jnp.where(y == sender, jnp.int32(len(receivers)), zero)
+    pl.semaphore_wait(bar, expected)
 
     for j in range(PER):
         pltpu.make_async_copy(send_u.at[s, j], recv_u.at[j, s], in_recv.at[j]).start()
@@ -162,11 +185,13 @@
 
         lax.fori_loop(1, S, spread_u, 0)
 
+    for copy in loads[2:]:
+        copy.wait()
+
     lane = lax.broadcasted_iota(jnp.int32, (L, HD), 1)
     tile = lax.broadcasted_iota(jnp.int32, (L, HD), 0) // 128
-    k_aug[:, HD:] = jnp.where(lane == tile, 1.0, 0.0).astype(BF16)
+    q_aug[:, HD:] = jnp.where(lane == tile, 1.0, 0.0).astype(BF16)
     v_aug[:, HD:] = jnp.ones((L, HD), BF16)
-    bias[...] = jnp.zeros((8, HD), F32)
     lane_row = lax.broadcasted_iota(jnp.int32, (HD, HD), 0)
     lane_col = lax.broadcasted_iota(jnp.int32, (HD, HD), 1)
     partner = jnp.where(lane_col % 2 == 0, lane_col + 1, lane_col - 1)
@@ -201,13 +226,18 @@
 
         fill(q_aug, qg_ref, factor)
         fill(k_aug, kg_ref, 1.0)
-        kept = mask_ref[head].astype(F32)
-        bias[:, 0:8] = (1.0 - kept) * NEG
+        masks = mask_ref[...].astype(F32)
+        of_head = lax.broadcasted_iota(jnp.int32, masks.shape, 2) == head
+        kept = jnp.sum(jnp.where(of_head, masks, 0.0), axis=2, keepdims=True)
+        lanes = lax.broadcasted_iota(jnp.int32, (8, HD), 1)
+        bias = jnp.zeros((8, HD), F32)
         for a in range(8):
-            q_aug[a * 128 : (a + 1) * 128, HD:] = jnp.broadcast_to(bias[a : a + 1, :], (128, HD)).astype(BF16)
-
-        gate_text = mod_ref[plan, 0, :, cols].astype(F32)[2:3] * step
-        gate_image = mod_ref[plan, 1, :, cols].astype(F32)[2:3] * step
+            bias = jnp.where(lanes == a, (1.0 - kept[a]) * NEG, bias)
+        for b in range(8):
+            k_aug[b * 128 : (b + 1) * 128, HD:] = jnp.broadcast_to(bias[b : b + 1, :], (128, HD)).astype(BF16)
+
+        gates = mod_ref[plan, 2, :, cols].astype(F32) * step
+        gate_text, gate_image = gates[0:1], gates[1:2]
 
         def rows_of(start, is_image):
             query = q_aug[pl.ds(start, QB), :]
@@ -232,6 +262,40 @@
         for n in range(HALF // QB):
             mine = pl.multiple_of(c * HALF + n * QB, QB)
             own[j, n * QB : (n + 1) * QB] = rows_of(mine, c == 1)
+
+    def chunk_of(i):
+        return lax.rem(i + x, NCH)
+
+    def both(j, r):
+        mine = own[j, pl.ds(pl.multiple_of(r * CH, CH), CH), :]
+        other = ex_in[j, r // 2, pl.ds(pl.multiple_of((r % 2) * CH, CH), CH), :].astype(F32)
+        return mine, other
+
+    def hop(src, dst, send_sem, recv_sem, to):
+        return pltpu.make_async_remote_copy(src, dst, send_sem, recv_sem, device_id=(to, s), device_id_type=MESH)
+
+    def push_copy(g, dst, recv, to):
+        return hop(c_out.at[g], dst.at[g], c_send.at[g], recv.at[g], 2 * to + c)
+
+    def pair_copy(g, n, dst, recv, to):
+        return hop(p_out.at[g], dst.at[g], p_send.at[n, g], recv.at[g], 2 * to + c)
+
+    def total_copy(g, n):
+        to = jnp.where(y == 3, 4 + n, 7 - n)
+        return hop(t_out.at[g], t_in.at[g], t_send.at[n, g], t_recv.at[g], 2 * to + c)
+
+    def got(recv, g):
+        hop(c_out.at[g], a_in.at[g], c_send.at[g], recv.at[g], tm).wait_recv()
+
+    def chunks(j, one_chunk):
+        def run(i, carry):
+            r = chunk_of(i)
+            one_chunk(r, j * NCH + r)
+            return carry
+
+        lax.fori_loop(0, NCH, run, 0)
+
+    def push(j):
         for n in range(HALF // QB):
             pltpu.make_async_remote_copy(
                 ex_out.at[j, n],
@@ -242,87 +306,60 @@
                 device_id_type=MESH,
             ).wait()
 
-    def chunk_of(i):
-        return lax.rem(i + x, NCH)
-
-    def both(j, r):
-        mine = own[j, pl.ds(pl.multiple_of(r * CH, CH), CH), :]
-        other = ex_in[j, r // 2, pl.ds(pl.multiple_of((r % 2) * CH, CH), CH), :].astype(F32)
-        return mine, other
-
-    def hop(src, dst, send_sem, recv_sem, to):
-        return pltpu.make_async_remote_copy(src, dst, send_sem, recv_sem, device_id=(to, s), device_id_type=MESH)
-
-    def forward_copy(g):
-        return hop(p_out.at[g], e_in.at[g], f_send.at[g], f_recv.at[g], tm + 2)
-
-    def reverse_copy(g):
-        return hop(s_out.at[g], r_in.at[g], r_send.at[g], r_recv.at[g], tm - 2)
-
-    def total_copy(src, g, n):
-        to = jnp.where(y == 3, 8 + 2 * n, 14 - 2 * n) + c
-        return hop(src.at[g], t_in.at[g], t_send.at[n, g], t_recv.at[g], to)
-
-    def forward(j):
-        def one_chunk(i, carry):
-            r = chunk_of(i)
-            g = j * NCH + r
+        def one_chunk(r, g):
             mine, other = both(j, r)
-            total = mine + other
-
-            @pl.when(ypos == 0)
+            c_out[g] = (mine + other).astype(BF16)
+            pl.when(ypos == 0)(lambda: push_copy(g, a_in, a_recv, y + 1).start())
+            pl.when(ypos == 2)(lambda: push_copy(g, b_in, b_recv, y + 1).start())
+            pl.when(y == 3)(lambda: push_copy(g, r_in, r_recv, y - 1).start())
+            pl.when(y == 1)(lambda: push_copy(g, a_in, a_recv, y - 1).start())
+
+        chunks(j, one_chunk)
+
+    def middle(j):
+        def one_chunk(r, g):
+            mine, other = both(j, r)
+
+            @pl.when(ypos == 1)
             def _():
-                p_out[g] = total.astype(BF16)
-
-            @pl.when(ypos > 0)
+                got(a_recv, g)
+                p_out[g] = (mine + other + a_in[g].astype(F32)).astype(BF16)
+                pair_copy(g, 0, a_in, a_recv, y + 1).start()
+                pair_copy(g, 1, a_in, a_recv, y + 2).start()
+
+            @pl.when(y == 2)
             def _():
-                forward_copy(g).wait_recv()
-                p_out[g] = (total + e_in[g].astype(F32)).astype(BF16)
-
-            @pl.when(ypos < 3)
-            def _():
-                forward_copy(g).start()
+                got(r_recv, g)
+                p_out[g] = (mine + other + r_in[g].astype(F32)).astype(BF16)
+                pair_copy(g, 0, r_in, r_recv, y - 2).start()
+
+        pl.when((ypos == 1) | (y == 2))(lambda: chunks(j, one_chunk))
+
+    def total(j):
+        def one_chunk(r, g):
+            mine, other = both(j, r)
+            got(a_recv, g)
+            before = mine + other + a_in[g].astype(F32)
 
             @pl.when(y == 3)
             def _():
-                total_copy(p_out, g, 0).start()
-                total_copy(p_out, g, 1).start()
-                s_out[g] = total.astype(BF16)
-                reverse_copy(g).start()
-
-            return carry
-
-        lax.fori_loop(0, NCH, one_chunk, 0)
-
-    def reverse(j):
-        @pl.when(y < 3)
-        def _():
-            def one_chunk(i, carry):
-                r = chunk_of(i)
-                g = j * NCH + r
-                mine, other = both(j, r)
-                reverse_copy(g).wait_recv()
-                s_out[g] = (mine + other + r_in[g].astype(F32)).astype(BF16)
-
-                @pl.when(y > 0)
-                def _():
-                    reverse_copy(g).start()
-
-                @pl.when(y == 0)
-                def _():
-                    total_copy(s_out, g, 0).start()
-                    total_copy(s_out, g, 1).start()
-
-                return carry
-
-            lax.fori_loop(0, NCH, one_chunk, 0)
+                got(b_recv, g)
+                t_out[g] = (before + b_in[g].astype(F32)).astype(BF16)
+
+            @pl.when(y == 0)
+            def _():
+                got(r_recv, g)
+                t_out[g] = (before + r_in[g].astype(F32)).astype(BF16)
+
+            total_copy(g, 0).start()
+            total_copy(g, 1).start()
+
+        chunks(j, one_chunk)
 
     def deliver(j):
         cols = pl.ds(pl.multiple_of((head0 + j) * HD, HD), HD)
 
-        def one_chunk(i, carry):
-            r = chunk_of(i)
-            g = j * NCH + r
+        def one_chunk(r, g):
             mine, other = both(j, r)
 
             def put(before):
@@ -331,25 +368,19 @@
                 d_out[0, g] = first.astype(BF16)
                 d_out[1, g] = after.astype(BF16)
 
-            @pl.when(y == 0)
-            def _():
-                put(jnp.zeros((CH, HD), F32))
-
-            @pl.when((y > 0) & (y < 4))
-            def _():
-                put(e_in[g].astype(F32))
-
-            @pl.when(y >= 4)
-            def _():
-                total_copy(p_out, g, 0).wait_recv()
-
-            @pl.when(y == 4)
-            def _():
-                put(t_in[g].astype(F32))
-
-            @pl.when(y > 4)
-            def _():
-                put(t_in[g].astype(F32) + e_in[g].astype(F32))
+            pl.when((ypos == 2) | (y == 7))(lambda: got(a_recv, g))
+            pl.when(y == 7)(lambda: got(b_recv, g))
+            pl.when(y >= 4)(lambda: got(t_recv, g))
+
+            def put_sum(*refs):
+                put(sum(ref[g].astype(F32) for ref in refs))
+
+            pl.when(y == 0)(lambda: put(jnp.zeros((CH, HD), F32)))
+            pl.when((y == 1) | (y == 2))(lambda: put_sum(a_in))
+            pl.when(y == 3)(lambda: put_sum(a_in, b_in))
+            pl.when(y == 4)(lambda: put_sum(t_in))
+            pl.when((y == 5) | (y == 6))(lambda: put_sum(t_in, a_in))
+            pl.when(y == 7)(lambda: put_sum(t_in, a_in, b_in))
 
             def piece(i, carry):
                 step_to = y * 2 + i // 4
@@ -371,48 +402,47 @@
                 return carry
 
             lax.fori_loop(0, 8, piece, 0)
-            return carry
-
-        lax.fori_loop(0, NCH, one_chunk, 0)
+
+        chunks(j, one_chunk)
 
     attention(0)
-    forward(0)
+    push(0)
+    pl.when(y == 1)(lambda: middle(0))
     attention(1)
-    forward(1)
-    reverse(0)
-
-    @pl.when(y < 4)
-    def _():
-        deliver(0)
-
+    pl.when((y == 2) | (y == 5))(lambda: middle(0))
+    pl.when(y == 3)(lambda: total(0))
+    push(1)
+    pl.when(y < 4)(lambda: deliver(0))
     attention(2)
-    forward(2)
-
-    @pl.when(y >= 4)
-    def _():
-        deliver(0)
-
-    reverse(1)
-    deliver(1)
-    reverse(2)
-    deliver(2)
+    pl.when(y == 1)(lambda: middle(1))
+    push(2)
+    pl.when((y == 2) | (y == 5))(lambda: middle(1))
+    pl.when(y == 0)(lambda: total(0))
+    pl.when(y == 3)(lambda: total(1))
+    pl.when(y >= 4)(lambda: deliver(0))
+    pl.when(y != 5)(lambda: deliver(1))
+    pl.when(y == 0)(lambda: deliver(2))
+    middle(2)
+    pl.when(y == 3)(lambda: total(2))
+    pl.when(y == 0)(lambda: total(1))
+    pl.when(y == 0)(lambda: total(2))
+    pl.when(y == 5)(lambda: deliver(1))
+    pl.when(y > 0)(lambda: deliver(2))
 
     sent = send_u.at[pl.ds(0, S - 1)]
     pltpu.make_async_copy(sent, sent, in_send).wait()
 
     def drain(g, carry):
-        @pl.when(ypos < 3)
-        def _():
-            forward_copy(g).wait_send()
-
-        @pl.when((y >= 1) & (y <= 3))
-        def _():
-            reverse_copy(g).wait_send()
+        pl.when((ypos == 0) | (ypos == 2) | (y == 1) | (y == 3))(
+            lambda: push_copy(g, a_in, a_recv, y).wait_send()
+        )
+        pl.when((ypos == 1) | (y == 2))(lambda: pair_copy(g, 0, a_in, a_recv, y).wait_send())
+        pl.when(ypos == 1)(lambda: pair_copy(g, 1, a_in, a_recv, y).wait_send())
 
         @pl.when((y == 0) | (y == 3))
         def _():
-            total_copy(p_out, g, 0).wait_send()
-            total_copy(p_out, g, 1).wait_send()
+            total_copy(g, 0).wait_send()
+            total_copy(g, 1).wait_send()
 
         return carry
 
@@ -438,24 +468,31 @@
 def body(trajectory, plan, step_sizes, modulation, q_gain, k_gain, tile_mask):
     cosine, sine = rope_tables()
     n = PER * NCH
-    vmem = pl.BlockSpec(memory_space=pltpu.VMEM)
     smem = pl.BlockSpec(memory_space=pltpu.SMEM)
     dma = pltpu.SemaphoreType.DMA
     blocks = pl.pallas_call(
         kernel,
         out_shape=jax.ShapeDtypeStruct((B, LOC, D), BF16),
-        in_specs=[smem, smem] + [vmem] * 7,
+        in_specs=[smem, smem] + [pl.BlockSpec(memory_space=pl.ANY)] * 7,
         out_specs=pl.BlockSpec(memory_space=pl.ANY),
         scratch_shapes=[
+            pltpu.VMEM((B, LOC, D), BF16),
+            pltpu.VMEM((modulation.shape[0], 3, 2, D), BF16),
+            pltpu.VMEM((2, D), F32),
+            pltpu.VMEM((2, D), F32),
+            pltpu.VMEM((L // 128, L // 128, H), jnp.int32),
+            pltpu.VMEM((L - TXT, HD), F32),
+            pltpu.VMEM((L - TXT, HD), F32),
             pltpu.VMEM((S, PER, LOC, HD), BF16),
             pltpu.VMEM((PER, S, LOC, HD), BF16),
             pltpu.VMEM((L, 2 * HD), BF16),
             pltpu.VMEM((L, 2 * HD), BF16),
             pltpu.VMEM((L, 2 * HD), BF16),
-            pltpu.VMEM((8, HD), F32),
             pltpu.VMEM((PER, HALF, HD), F32),
             pltpu.VMEM((PER, HALF // QB, QB, HD), BF16),
             pltpu.VMEM((PER, HALF // QB, QB, HD), BF16),
+            pltpu.VMEM((n, CH, HD), BF16),
+            pltpu.VMEM((n, CH, HD), BF16),
             pltpu.VMEM((n, CH, HD), BF16),
             pltpu.VMEM((n, CH, HD), BF16),
             pltpu.VMEM((n, CH, HD), BF16),
@@ -470,15 +507,17 @@
             dma((n,)),
             dma((n,)),
             dma((n,)),
+            dma((n,)),
             dma((2, n)),
-            dma((n,)),
+            dma((2, n)),
             dma,
             dma,
+            dma((7,)),
         ],
         compiler_params=pltpu.CompilerParams(
             collective_id=0, has_side_effects=True, vmem_limit_bytes=56 * 1024 * 1024
         ),
-    )(plan, step_sizes, trajectory[0], modulation, q_gain, k_gain, tile_mask, jnp.asarray(cosine), jnp.asarray(sine))
+    )(plan, step_sizes, trajectory[0], modulation.transpose(0, 2, 1, 3), q_gain, k_gain, tile_mask.transpose(1, 2, 0), jnp.asarray(cosine), jnp.asarray(sine))
     return blocks.astype(F32)[None]
 
 

time: 94.2 us -> 68.3 us (0.73)
  the two profiles are of different devices: /device:TPU:49 before, /device:TPU:41 now
where the time goes in v2:
time: 68.3 us; the launch traced here: 68.1 us
  Pallas kernels  64.4 us (94%)
  other arithmetic  2.43 us (4%)
  between operations  1.3 us (2%)
    pallas_call x1, Pallas kernels, body(): pl.pallas_call(kernel, out_shape=jax.ShapeDtypeStruct((B, LOC, D), BF16),...  64.4 us
    broadcast_in_dim x1, other arithmetic, body(): return blocks.astype(F32)[None]  2.43 us

profile of v2, /device:TPU:41, one launch (start us, length us, event | category | flops | bytes accessed | tf_op | source)
XLA Modules:
  0.0 68.1 jit_solution(15120257937577016215)
XLA Ops:
  1.3 64.4 %shard_map.91 = bf16[4,32,3072]{2,1,0:T(8,128)(2,1)} custom-call(s32[1]{0:T(128)S(6)} %copy.10.plan_ref, f32[1]{0:T(128)S(6)} %copy.11.step_ref, bf16[4,32,3072]{2,1,0:T(8,128)(2,1)} %bitcast.6, bf16[16,3,2,3072]{3,2,1,0:T(2,128)(2,1)} %bitcast.7, f32[2,3072]{1,0:T(2,128)} %qg_hbm.1, f32[2,3072]{1,0:T(2,128)} %kg_hbm.1, s32[8,8,24]{2,1,0:T(8,128)} %bitcast.8, ...), custom_call_target="tpu_custom_call" | custom-call | tf_op jit(solution)/shard_map/pallas_call | solution.py:473
  65.7 2.4 %bitcast_convert_fusion = f32[1,4,32,3072]{3,2,1,0:T(8,128)} fusion(bf16[4,32,3072]{2,1,0:T(8,128)(2,1)} %shard_map.91), kind=kLoop, calls=%fused_computation | loop fusion | flops 393216 | bytes 2359296 | tf_op jit(solution)/shard_map/broadcast_in_dim | solution.py:521

commit v3 on v2

--- a/solution.py
+++ b/solution.py
@@ -23,10 +23,9 @@
 HALF = L // 2
 CH = 128
 NCH = HALF // CH
-QB = 256
 NEG = -1e30
 
-TO = {0: (1, 6, 7), 1: (0, 2, 3), 2: (0, 3), 3: (2, 4, 5), 4: (5,), 5: (6, 7), 6: (7,)}
+TO = {0: (1,), 1: (2, 3, 6, 7), 2: (1, 3), 3: (1, 4, 5), 4: (5,), 5: (6, 7), 6: (7,)}
 
 
 def rope_tables():
@@ -204,6 +203,16 @@
         row = jnp.broadcast_to(row, (8, HD))
         return jnp.where(even, pltpu.roll(row, HD - 1, 1), pltpu.roll(row, 1, 1))[0:1]
 
+    def ex_copy(j):
+        return pltpu.make_async_remote_copy(
+            ex_out.at[j],
+            ex_in.at[j],
+            ex_send.at[j],
+            ex_recv.at[j],
+            device_id=(y * 2 + 1 - c, s),
+            device_id_type=MESH,
+        )
+
     def attention(j):
         head = head0 + j
         cols = pl.ds(pl.multiple_of(head * HD, HD), HD)
@@ -239,36 +248,30 @@
         gates = mod_ref[plan, 2, :, cols].astype(F32) * step
         gate_text, gate_image = gates[0:1], gates[1:2]
 
-        def rows_of(start, is_image):
-            query = q_aug[pl.ds(start, QB), :]
+        def rows_of(core):
+            first = (1 - core) * (TXT // 2)
+            text = pl.ds(pl.multiple_of(first, TXT // 2), TXT // 2)
+            picture = pl.ds(pl.multiple_of(TXT + first, TXT // 2), TXT // 2)
+            query = jnp.concatenate([q_aug[text, :], q_aug[picture, :]], axis=0)
             scores = lax.dot_general(query, k_aug[...], (((1,), (1,)), ((), ())), preferred_element_type=F32)
             top = jnp.max(scores, axis=-1, keepdims=True)
             weights = jnp.exp2(scores - top).astype(BF16)
             summed = jnp.dot(weights, v_aug[...], preferred_element_type=F32)
-            gate = jnp.where(is_image, gate_image, gate_text)
-            return (summed[:, :HD] / summed[:, HD:]) * gate
-
-        for n in range(HALF // QB):
-            theirs = pl.multiple_of((1 - c) * HALF + n * QB, QB)
-            ex_out[j, n] = rows_of(theirs, c == 0).astype(BF16)
-            pltpu.make_async_remote_copy(
-                ex_out.at[j, n],
-                ex_in.at[j, n],
-                ex_send.at[j, n],
-                ex_recv.at[j, n],
-                device_id=(y * 2 + 1 - c, s),
-                device_id_type=MESH,
-            ).start()
-        for n in range(HALF // QB):
-            mine = pl.multiple_of(c * HALF + n * QB, QB)
-            own[j, n * QB : (n + 1) * QB] = rows_of(mine, c == 1)
+            result = summed[:, :HD] / summed[:, HD:]
+            return result[: TXT // 2] * gate_text, result[TXT // 2 :] * gate_image
+
+        for n, part in enumerate(rows_of(1 - c)):
+            ex_out[j, n * (HALF // 2) : (n + 1) * (HALF // 2)] = part.astype(BF16)
+        ex_copy(j).start()
+        for n, part in enumerate(rows_of(c)):
+            own[j, n * (HALF // 2) : (n + 1) * (HALF // 2)] = part
 
     def chunk_of(i):
-        return lax.rem(i + x, NCH)
+        return i // 2 * 2 + lax.rem(i + x, 2)
 
     def both(j, r):
         mine = own[j, pl.ds(pl.multiple_of(r * CH, CH), CH), :]
-        other = ex_in[j, r // 2, pl.ds(pl.multiple_of((r % 2) * CH, CH), CH), :].astype(F32)
+        other = ex_in[j, pl.ds(pl.multiple_of(r * CH, CH), CH), :].astype(F32)
         return mine, other
 
     def hop(src, dst, send_sem, recv_sem, to):
@@ -277,86 +280,97 @@
     def push_copy(g, dst, recv, to):
         return hop(c_out.at[g], dst.at[g], c_send.at[g], recv.at[g], 2 * to + c)
 
+    def back_copy(g):
+        return hop(c_out.at[g], b_in.at[g], p_send.at[0, g], b_recv.at[g], 2 * (y - 1) + c)
+
     def pair_copy(g, n, dst, recv, to):
         return hop(p_out.at[g], dst.at[g], p_send.at[n, g], recv.at[g], 2 * to + c)
 
     def total_copy(g, n):
-        to = jnp.where(y == 3, 4 + n, 7 - n)
+        to = jnp.where(y == 3, 5 - n, 7 - n)
         return hop(t_out.at[g], t_in.at[g], t_send.at[n, g], t_recv.at[g], 2 * to + c)
 
     def got(recv, g):
         hop(c_out.at[g], a_in.at[g], c_send.at[g], recv.at[g], tm).wait_recv()
 
-    def chunks(j, one_chunk):
+    def chunks(j, one_chunk, low=0, high=NCH):
         def run(i, carry):
             r = chunk_of(i)
             one_chunk(r, j * NCH + r)
             return carry
 
-        lax.fori_loop(0, NCH, run, 0)
+        lax.fori_loop(low, high, run, 0)
+
+    sides = ((0, NCH // 2), (NCH // 2, NCH))
 
     def push(j):
-        for n in range(HALF // QB):
-            pltpu.make_async_remote_copy(
-                ex_out.at[j, n],
-                ex_in.at[j, n],
-                ex_send.at[j, n],
-                ex_recv.at[j, n],
-                device_id=(y * 2 + 1 - c, s),
-                device_id_type=MESH,
-            ).wait()
+        ex_copy(j).wait()
 
         def one_chunk(r, g):
             mine, other = both(j, r)
             c_out[g] = (mine + other).astype(BF16)
             pl.when(ypos == 0)(lambda: push_copy(g, a_in, a_recv, y + 1).start())
+            pl.when(y == 2)(lambda: back_copy(g).start())
             pl.when(ypos == 2)(lambda: push_copy(g, b_in, b_recv, y + 1).start())
-            pl.when(y == 3)(lambda: push_copy(g, r_in, r_recv, y - 1).start())
-            pl.when(y == 1)(lambda: push_copy(g, a_in, a_recv, y - 1).start())
+            pl.when(y == 3)(lambda: push_copy(g, r_in, r_recv, y - 2).start())
 
         chunks(j, one_chunk)
 
-    def middle(j):
-        def one_chunk(r, g):
-            mine, other = both(j, r)
-
-            @pl.when(ypos == 1)
-            def _():
-                got(a_recv, g)
-                p_out[g] = (mine + other + a_in[g].astype(F32)).astype(BF16)
-                pair_copy(g, 0, a_in, a_recv, y + 1).start()
-                pair_copy(g, 1, a_in, a_recv, y + 2).start()
-
-            @pl.when(y == 2)
-            def _():
-                got(r_recv, g)
-                p_out[g] = (mine + other + r_in[g].astype(F32)).astype(BF16)
-                pair_copy(g, 0, r_in, r_recv, y - 2).start()
-
-        pl.when((ypos == 1) | (y == 2))(lambda: chunks(j, one_chunk))
-
-    def total(j):
+    def middle_chunk(j):
         def one_chunk(r, g):
             mine, other = both(j, r)
             got(a_recv, g)
-            before = mine + other + a_in[g].astype(F32)
+            p_out[g] = (mine + other + a_in[g].astype(F32)).astype(BF16)
+            pair_copy(g, 0, a_in, a_recv, y + 2).start()
+
+        return one_chunk
+
+    def middle_rest(j, side):
+        chunks(j, lambda r, g: pair_copy(g, 1, a_in, a_recv, y + 1).start(), *side)
+
+    def middle(j):
+        for side in sides:
+            chunks(j, middle_chunk(j), *side)
+            middle_rest(j, side)
+
+    def total_chunk(j):
+        def one_chunk(r, g):
+            mine, other = both(j, r)
+            pl.when(y == 3)(lambda: got(a_recv, g))
+            got(b_recv, g)
+            before = mine + other + a_in[g].astype(F32) + b_in[g].astype(F32)
 
             @pl.when(y == 3)
             def _():
-                got(b_recv, g)
-                t_out[g] = (before + b_in[g].astype(F32)).astype(BF16)
-
-            @pl.when(y == 0)
+                t_out[g] = before.astype(BF16)
+
+            @pl.when(y == 1)
             def _():
                 got(r_recv, g)
                 t_out[g] = (before + r_in[g].astype(F32)).astype(BF16)
 
             total_copy(g, 0).start()
-            total_copy(g, 1).start()
-
-        chunks(j, one_chunk)
-
-    def deliver(j):
+
+        return one_chunk
+
+    def total_rest(j, side):
+        chunks(j, lambda r, g: total_copy(g, 1).start(), *side)
+
+    def total(j):
+        for side in sides:
+            chunks(j, total_chunk(j), *side)
+            total_rest(j, side)
+
+    def at_once(j, first, k, second, side):
+        def run(i, carry):
+            r = chunk_of(i)
+            first(r, j * NCH + r)
+            second(r, k * NCH + r)
+            return carry
+
+        lax.fori_loop(side[0], side[1], run, 0)
+
+    def deliver_chunk(j):
         cols = pl.ds(pl.multiple_of((head0 + j) * HD, HD), HD)
 
         def one_chunk(r, g):
@@ -384,7 +398,7 @@
 
             def piece(i, carry):
                 step_to = y * 2 + i // 4
-                shard = c * (S // 2) + r * 4 + lax.rem(i + s // 4, 4)
+                shard = r // 2 * (S // 2) + (1 - c) * (S // 4) + r % 2 * 4 + lax.rem(i + s // 4, 4)
                 src = d_out.at[i // 4, g, pl.ds(pl.multiple_of(lax.rem(i + s // 4, 4) * LOC, LOC), LOC)]
                 dst = out_ref.at[image, :, cols]
                 here = (shard == s) & (step_to == tm)
@@ -403,43 +417,57 @@
 
             lax.fori_loop(0, 8, piece, 0)
 
-        chunks(j, one_chunk)
+        return one_chunk
+
+    def deliver(j):
+        chunks(j, deliver_chunk(j))
 
     attention(0)
     push(0)
     pl.when(y == 1)(lambda: middle(0))
     attention(1)
-    pl.when((y == 2) | (y == 5))(lambda: middle(0))
-    pl.when(y == 3)(lambda: total(0))
     push(1)
-    pl.when(y < 4)(lambda: deliver(0))
+    pl.when(y == 5)(lambda: middle(0))
+    pl.when((y == 1) | (y == 3))(lambda: total(0))
+    pl.when((y < 2) | (y == 3))(lambda: deliver(0))
     attention(2)
     pl.when(y == 1)(lambda: middle(1))
     push(2)
-    pl.when((y == 2) | (y == 5))(lambda: middle(1))
-    pl.when(y == 0)(lambda: total(0))
-    pl.when(y == 3)(lambda: total(1))
-    pl.when(y >= 4)(lambda: deliver(0))
-    pl.when(y != 5)(lambda: deliver(1))
-    pl.when(y == 0)(lambda: deliver(2))
-    middle(2)
-    pl.when(y == 3)(lambda: total(2))
-    pl.when(y == 0)(lambda: total(1))
-    pl.when(y == 0)(lambda: total(2))
-    pl.when(y == 5)(lambda: deliver(1))
-    pl.when(y > 0)(lambda: deliver(2))
+
+    @pl.when(y == 1)
+    def _():
+        for side in sides:
+            at_once(1, total_chunk(1), 2, middle_chunk(2), side)
+            total_rest(1, side)
+            middle_rest(2, side)
+
+    @pl.when(y == 3)
+    def _():
+        for j in (1, 2):
+            for side in sides:
+                at_once(j, total_chunk(j), j, deliver_chunk(j), side)
+                total_rest(j, side)
+
+    pl.when((y == 2) | (y >= 4))(lambda: deliver(0))
+
+    @pl.when(y == 5)
+    def _():
+        middle(1)
+        middle(2)
+
+    pl.when(y != 3)(lambda: deliver(1))
+    pl.when(y == 1)(lambda: total(2))
+    pl.when(y != 3)(lambda: deliver(2))
 
     sent = send_u.at[pl.ds(0, S - 1)]
     pltpu.make_async_copy(sent, sent, in_send).wait()
 
     def drain(g, carry):
-        pl.when((ypos == 0) | (ypos == 2) | (y == 1) | (y == 3))(
-            lambda: push_copy(g, a_in, a_recv, y).wait_send()
-        )
+        pl.when((ypos == 0) | (ypos == 2) | (y == 3))(lambda: push_copy(g, a_in, a_recv, y).wait_send())
         pl.when((ypos == 1) | (y == 2))(lambda: pair_copy(g, 0, a_in, a_recv, y).wait_send())
         pl.when(ypos == 1)(lambda: pair_copy(g, 1, a_in, a_recv, y).wait_send())
 
-        @pl.when((y == 0) | (y == 3))
+        @pl.when((y == 1) | (y == 3))
         def _():
             total_copy(g, 0).wait_send()
             total_copy(g, 1).wait_send()
@@ -452,7 +480,7 @@
     pltpu.make_async_copy(most, most, o_send).wait()
     rest = d_out.at[0, :, pl.ds(0, LOC)]
     last = d_out.at[0, pl.ds(0, 9), pl.ds(0, LOC)]
-    holds_own = c == s // (S // 2)
+    holds_own = 1 - c == s // (S // 4) % 2
 
     @pl.when(holds_own)
     def _():
@@ -489,8 +517,8 @@
             pltpu.VMEM((L, 2 * HD), BF16),
             pltpu.VMEM((L, 2 * HD), BF16),
             pltpu.VMEM((PER, HALF, HD), F32),
-            pltpu.VMEM((PER, HALF // QB, QB, HD), BF16),
-            pltpu.VMEM((PER, HALF // QB, QB, HD), BF16),
+            pltpu.VMEM((PER, HALF, HD), BF16),
+            pltpu.VMEM((PER, HALF, HD), BF16),
             pltpu.VMEM((n, CH, HD), BF16),
             pltpu.VMEM((n, CH, HD), BF16),
             pltpu.VMEM((n, CH, HD), BF16),
@@ -501,8 +529,8 @@
             pltpu.VMEM((2, n, CH, HD), BF16),
             dma,
             dma((PER,)),
-            dma((PER, HALF // QB)),
-            dma((PER, HALF // QB)),
+            dma((PER,)),
+            dma((PER,)),
             dma((n,)),
             dma((n,)),
             dma((n,)),

time: 68.3 us -> 64.6 us (0.946)
  the two profiles are of different devices: /device:TPU:41 before, /device:TPU:49 now
where the time goes in v3:
time: 64.6 us; the launch traced here: 64.4 us
  Pallas kernels  60.7 us (94%)
  other arithmetic  2.43 us (4%)
  between operations  1.3 us (2%)
    pallas_call x1, Pallas kernels, body(): pl.pallas_call(kernel, out_shape=jax.ShapeDtypeStruct((B, LOC, D), BF16),...  60.7 us
    broadcast_in_dim x1, other arithmetic, body(): return blocks.astype(F32)[None]  2.43 us

profile of v3, /device:TPU:49, one launch (start us, length us, event | category | flops | bytes accessed | tf_op | source)
XLA Modules:
  0.0 64.4 jit_solution(14862696446540730178)
XLA Ops:
  1.3 60.7 %shard_map.91 = bf16[4,32,3072]{2,1,0:T(8,128)(2,1)} custom-call(s32[1]{0:T(128)S(6)} %copy.10.plan_ref, f32[1]{0:T(128)S(6)} %copy.11.step_ref, bf16[4,32,3072]{2,1,0:T(8,128)(2,1)} %bitcast.6, bf16[16,3,2,3072]{3,2,1,0:T(2,128)(2,1)} %bitcast.7, f32[2,3072]{1,0:T(2,128)} %qg_hbm.1, f32[2,3072]{1,0:T(2,128)} %kg_hbm.1, s32[8,8,24]{2,1,0:T(8,128)} %bitcast.8, ...), custom_call_target="tpu_custom_call" | custom-call | tf_op jit(solution)/shard_map/pallas_call | solution.py:501
  62.0 2.4 %bitcast_convert_fusion = f32[1,4,32,3072]{3,2,1,0:T(8,128)} fusion(bf16[4,32,3072]{2,1,0:T(8,128)(2,1)} %shard_map.91), kind=kLoop, calls=%fused_computation | loop fusion | flops 393216 | bytes 2359296 | tf_op jit(solution)/shard_map/broadcast_in_dim | solution.py:549

commit v4 on v3

--- a/solution.py
+++ b/solution.py
@@ -1,5 +1,3 @@
-import functools
-
 import jax
 import jax.numpy as jnp
 import numpy as np
@@ -350,16 +348,13 @@
                 t_out[g] = (before + r_in[g].astype(F32)).astype(BF16)
 
             total_copy(g, 0).start()
+            total_copy(g, 1).start()
 
         return one_chunk
-
-    def total_rest(j, side):
-        chunks(j, lambda r, g: total_copy(g, 1).start(), *side)
 
     def total(j):
         for side in sides:
             chunks(j, total_chunk(j), *side)
-            total_rest(j, side)
 
     def at_once(j, first, k, second, side):
         def run(i, carry):
@@ -426,11 +421,13 @@
     push(0)
     pl.when(y == 1)(lambda: middle(0))
     attention(1)
+    pl.when(y == 3)(lambda: total(0))
     push(1)
     pl.when(y == 5)(lambda: middle(0))
-    pl.when((y == 1) | (y == 3))(lambda: total(0))
-    pl.when((y < 2) | (y == 3))(lambda: deliver(0))
+    pl.when(y == 1)(lambda: total(0))
+    pl.when((y == 0) | (y == 1) | (y == 2) | (y == 3))(lambda: deliver(0))
     attention(2)
+    pl.when((y == 4) | (y == 5) | (y == 6) | (y == 7))(lambda: deliver(0))
     pl.when(y == 1)(lambda: middle(1))
     push(2)
 
@@ -438,7 +435,6 @@
     def _():
         for side in sides:
             at_once(1, total_chunk(1), 2, middle_chunk(2), side)
-            total_rest(1, side)
             middle_rest(2, side)
 
     @pl.when(y == 3)
@@ -446,9 +442,7 @@
         for j in (1, 2):
             for side in sides:
                 at_once(j, total_chunk(j), j, deliver_chunk(j), side)
-                total_rest(j, side)
-
-    pl.when((y == 2) | (y >= 4))(lambda: deliver(0))
+
 
     @pl.when(y == 5)
     def _():

time: 64.6 us -> 63.6 us (0.985)
  the two profiles are of different devices: /device:TPU:49 before, /device:TPU:169 now
where the time goes in v4:
time: 63.6 us; the launch traced here: 63.4 us
  Pallas kernels  59.6 us (94%)
  other arithmetic  2.43 us (4%)
  between operations  1.3 us (2%)
    pallas_call x1, Pallas kernels, body(): pl.pallas_call(kernel, out_shape=jax.ShapeDtypeStruct((B, LOC, D), BF16),...  59.6 us
    broadcast_in_dim x1, other arithmetic, body(): return blocks.astype(F32)[None]  2.43 us

profile of v4, /device:TPU:169, one launch (start us, length us, event | category | flops | bytes accessed | tf_op | source)
XLA Modules:
  0.0 63.4 jit_solution(15398728565344372390)
XLA Ops:
  1.3 59.6 %shard_map.91 = bf16[4,32,3072]{2,1,0:T(8,128)(2,1)} custom-call(s32[1]{0:T(128)S(6)} %copy.10.plan_ref, f32[1]{0:T(128)S(6)} %copy.11.step_ref, bf16[4,32,3072]{2,1,0:T(8,128)(2,1)} %bitcast.6, bf16[16,3,2,3072]{3,2,1,0:T(2,128)(2,1)} %bitcast.7, f32[2,3072]{1,0:T(2,128)} %qg_hbm.1, f32[2,3072]{1,0:T(2,128)} %kg_hbm.1, s32[8,8,24]{2,1,0:T(8,128)} %bitcast.8, ...), custom_call_target="tpu_custom_call" | custom-call | tf_op jit(solution)/shard_map/pallas_call | solution.py:495
  60.9 2.4 %bitcast_convert_fusion = f32[1,4,32,3072]{3,2,1,0:T(8,128)} fusion(bf16[4,32,3072]{2,1,0:T(8,128)(2,1)} %shard_map.91), kind=kLoop, calls=%fused_computation | loop fusion | flops 393216 | bytes 2359296 | tf_op jit(solution)/shard_map/broadcast_in_dim | solution.py:543

commit v5 on v4

--- a/solution.py
+++ b/solution.py
@@ -447,9 +447,11 @@
     @pl.when(y == 5)
     def _():
         middle(1)
-        middle(2)
-
-    pl.when(y != 3)(lambda: deliver(1))
+        for side in sides:
+            at_once(2, middle_chunk(2), 1, deliver_chunk(1), side)
+            middle_rest(2, side)
+
+    pl.when((y != 3) & (y != 5))(lambda: deliver(1))
     pl.when(y == 1)(lambda: total(2))
     pl.when(y != 3)(lambda: deliver(2))
 
@@ -485,6 +487,19 @@
         pltpu.make_async_copy(rest, rest, o_send).wait()
 
     pltpu.make_async_copy(out_ref, out_ref, o_recv).wait()
+
+
+def widen(src, dst, narrow, wide, read, write):
+    ins = [pltpu.make_async_copy(src.at[b], narrow.at[b], read.at[b]) for b in range(B)]
+    outs = [pltpu.make_async_copy(wide.at[b], dst.at[b], write.at[b]) for b in range(B)]
+    for copy in ins:
+        copy.start()
+    for b in range(B):
+        ins[b].wait()
+        wide[b] = narrow[b].astype(F32)
+        outs[b].start()
+    for copy in outs:
+        copy.wait()
 
 
 def body(trajectory, plan, step_sizes, modulation, q_gain, k_gain, tile_mask):
@@ -540,7 +555,15 @@
             collective_id=0, has_side_effects=True, vmem_limit_bytes=56 * 1024 * 1024
         ),
     )(plan, step_sizes, trajectory[0], modulation.transpose(0, 2, 1, 3), q_gain, k_gain, tile_mask.transpose(1, 2, 0), jnp.asarray(cosine), jnp.asarray(sine))
-    return blocks.astype(F32)[None]
+    result = pl.pallas_call(
+        widen,
+        out_shape=jax.ShapeDtypeStruct((B, LOC, D), F32),
+        in_specs=[pl.BlockSpec(memory_space=pl.ANY)],
+        out_specs=pl.BlockSpec(memory_space=pl.ANY),
+        scratch_shapes=[pltpu.VMEM((B, LOC, D), BF16), pltpu.VMEM((B, LOC, D), F32), dma((B,)), dma((B,))],
+        compiler_params=pltpu.CompilerParams(vmem_limit_bytes=56 * 1024 * 1024),
+    )(blocks)
+    return result[None]
 
 
 def solution(mesh):

time: 63.6 us -> 63.3 us (level)
  other arithmetic: 2.43 us -> 0 us
  Pallas kernels: 59.6 us -> 61.8 us
    broadcast_in_dim x1 -> x0, other arithmetic: 2.43 us -> none  [body(): return blocks.astype(F32)[None]]
    pallas_call x0 -> x1, Pallas kernels: none -> 2.16 us  [body(): pl.pallas_call(widen, out_shape=jax.ShapeDtypeStruct((B, LOC, D), F32), i...]
where the time goes in v5:
time: 63.3 us; the launch traced here: 63.1 us
  Pallas kernels  61.8 us (98%)
  between operations  1.3 us (2%)
    pallas_call x1, Pallas kernels, body(): pl.pallas_call(kernel, out_shape=jax.ShapeDtypeStruct((B, LOC, D), BF16),...  59.6 us
    pallas_call x1, Pallas kernels, body(): pl.pallas_call(widen, out_shape=jax.ShapeDtypeStruct((B, LOC, D), F32), i...  2.16 us

profile of v5, /device:TPU:169, one launch (start us, length us, event | category | flops | bytes accessed | tf_op | source)
XLA Modules:
  0.0 63.1 jit_solution(2488426748161243591)
XLA Ops:
  1.3 59.6 %shard_map.91.src = bf16[4,32,3072]{2,1,0:T(8,128)(2,1)} custom-call(s32[1]{0:T(128)S(6)} %copy.10.plan_ref, f32[1]{0:T(128)S(6)} %copy.11.step_ref, bf16[4,32,3072]{2,1,0:T(8,128)(2,1)} %bitcast.4, bf16[16,3,2,3072]{3,2,1,0:T(2,128)(2,1)} %bitcast.5, f32[2,3072]{1,0:T(2,128)} %qg_hbm.1, f32[2,3072]{1,0:T(2,128)} %kg_hbm.1, s32[8,8,24]{2,1,0:T(8,128)} %bitcast.6, ...), custom_call_target="tpu_custom_call" | custom-call | tf_op jit(solution)/shard_map/pallas_call | solution.py:510
  60.9 2.2 %shard_map.92 = f32[4,32,3072]{2,1,0:T(8,128)} custom-call(bf16[4,32,3072]{2,1,0:T(8,128)(2,1)} %shard_map.91.src), custom_call_target="tpu_custom_call" | custom-call | tf_op jit(solution)/shard_map/pallas_call | solution.py:558
